TPU v7x, 32 devices: a whole 2x2x4 slice. The times are simulated.
32 devices in a mesh: sub: 8 (over z, x), grp: 4 (over y, core).
Axes of the slice: x: 2, y: 2, z: 4, core: 2. Of those that a mesh axis runs over, the one named last changes fastest.
Arguments:
- right_side: float32 [65536, 128], P(('sub', 'grp')), may hold values from -6 to 6
- noise_var: float32 [65536], P(('sub', 'grp')), may hold values from 0.5 to 2
- near_tiles: bfloat16 [256, 6, 256, 256], P(('sub', 'grp')), may hold values from -0.15625 to 0.15625
- near_index: int32 [256, 6], P(('sub', 'grp')), may hold values from 0 to 255, as said below
- leaf_basis: bfloat16 [256, 64, 256], P(('sub', 'grp')), may hold values from -0.375 to 0.375
- leaf_transfer: bfloat16 [256, 64, 64], P(('sub', 'grp')), may hold values from -0.4375 to 0.4375
- leaf_coupling: bfloat16 [256, 4, 64, 64], P(('sub', 'grp')), may hold values from -0.375 to 0.375
- far_leaf: int32 [256, 4], P(('sub', 'grp')), may hold values from 0 to 255, as said below
- dev_transfer: bfloat16 [32, 64, 64], P(('sub', 'grp')), may hold values from -0.4375 to 0.4375
- dev_coupling: bfloat16 [32, 4, 64, 64], P(('sub', 'grp')), may hold values from -0.375 to 0.375
- far_dev: int32 [32, 4], P(('sub', 'grp')), may hold values from 0 to 31, as said below
- mid_coupling: bfloat16 [4, 3, 64, 64], P('grp'), may hold values from -0.4375 to 0.4375
- far_mid: int32 [4, 3], P('grp'), may hold values from 0 to 3, as said below
Outputs:
- solution: float32 [65536, 128], P(('sub', 'grp'))
Inputs may be any that keep to these rules, and one draw needn't show every extreme that they name: `near_index`: row l lists 6 different leaves, l itself among them, each within 6 leaves of l in the periodic leaf order (leaf indices taken modulo 256). `far_leaf`: row l lists 4 different leaves within 6 leaves of l in the periodic leaf order, none of them in row l of near_index. `far_dev`: row d lists 4 different subtrees other than d, each of the same group as d. `far_mid`: row m lists 3 different mid nodes other than m.
All inputs are finite; a program needn't handle non-finite values.
Results may differ from a plain program's by a relative error of at most 0.025.
Values may be sent and summed in bfloat16 or wider, within the bound.
A program may use at most 64 MiB of HBM per device.

v0:
```python
import jax
import jax.numpy as jnp
from jax import lax
from jax.sharding import PartitionSpec as P

SPAN = 6
ITERS = 4


relax_step = 0.3


def from_behind(value, axis, steps):
    count = lax.axis_size(axis)
    pairs = [(source, (source + steps) % count) for source in range(count)]
    return lax.ppermute(value, axis, pairs)


def per_device(
    right_side,
    noise_var,
    near_tiles,
    near_index,
    leaf_basis,
    leaf_transfer,
    leaf_coupling,
    far_leaf,
    dev_transfer,
    dev_coupling,
    far_dev,
    mid_coupling,
    far_mid,
):
    leaves_dev = near_tiles.shape[0]
    leaf_size = near_tiles.shape[2]
    probes = right_side.shape[1]
    rank_size = leaf_basis.shape[1]
    groups = lax.axis_size("grp")
    group_devs = lax.axis_size("sub")
    total_leaves = leaves_dev * groups * group_devs
    sub_index = lax.axis_index("sub")
    device = sub_index * groups + lax.axis_index("grp")
    first_leaf = device * leaves_dev
    near_local = jnp.mod(near_index - first_leaf + SPAN, total_leaves)
    far_local = jnp.mod(far_leaf - first_leaf + SPAN, total_leaves)
    far_within = far_dev[0] // groups
    mid_local = sub_index // 8
    own_mid_coupling = lax.dynamic_index_in_dim(mid_coupling, mid_local, 0, keepdims=False)
    own_far_mid = lax.dynamic_index_in_dim(far_mid, mid_local, 0, keepdims=False)
    own_transfer = dev_transfer[0]
    iterate = relax_step * right_side
    for sweep in range(ITERS):
        rounded = iterate.astype(jnp.bfloat16).reshape(leaves_dev, leaf_size, probes)
        leaf_coef = jnp.einsum(
            "lrj,ljp->lrp", leaf_basis, rounded, preferred_element_type=jnp.float32
        ).astype(jnp.bfloat16)
        below_vec, below_coef = from_behind(
            (rounded[leaves_dev - SPAN :], leaf_coef[leaves_dev - SPAN :]), ("sub", "grp"), 1
        )
        above_vec, above_coef = from_behind((rounded[:SPAN], leaf_coef[:SPAN]), ("sub", "grp"), -1)
        dev_coef = jnp.einsum(
            "lrs,lsp->rp", leaf_transfer, leaf_coef, preferred_element_type=jnp.float32
        ).astype(jnp.bfloat16)
        lifted = jnp.dot(own_transfer, dev_coef, preferred_element_type=jnp.float32).astype(
            jnp.bfloat16
        )
        group_coef = lax.all_gather(dev_coef[None], "sub", axis=0, tiled=True)
        group_lifted = lax.all_gather(lifted[None], "sub", axis=0, tiled=True)
        own_mids = (
            group_lifted.astype(jnp.float32)
            .reshape(group_devs // 8, 8, rank_size, probes)
            .sum(1)
            .astype(jnp.bfloat16)
        )
        mid_coef = lax.all_gather(own_mids, "grp", axis=0, tiled=True)
        mid_field = jnp.einsum(
            "krs,ksp->rp",
            own_mid_coupling,
            jnp.take(mid_coef, own_far_mid, axis=0),
            preferred_element_type=jnp.float32,
        ).astype(jnp.bfloat16)
        dev_field = jnp.einsum(
            "krs,ksp->rp",
            dev_coupling[0],
            jnp.take(group_coef, far_within, axis=0),
            preferred_element_type=jnp.float32,
        )
        dev_field = (
            dev_field + jnp.dot(own_transfer.T, mid_field, preferred_element_type=jnp.float32)
        ).astype(jnp.bfloat16)
        window_vec = jnp.concatenate([below_vec, rounded, above_vec], axis=0)
        window_coef = jnp.concatenate([below_coef, leaf_coef, above_coef], axis=0)
        leaf_field = jnp.einsum(
            "lkrs,lksp->lrp",
            leaf_coupling,
            jnp.take(window_coef, far_local, axis=0),
            preferred_element_type=jnp.float32,
        )
        leaf_field = (
            leaf_field
            + jnp.einsum(
                "lrs,rp->lsp", leaf_transfer, dev_field, preferred_element_type=jnp.float32
            )
        ).astype(jnp.bfloat16)
        far_part = jnp.einsum(
            "lrj,lrp->ljp", leaf_basis, leaf_field, preferred_element_type=jnp.float32
        )
        near_part = jnp.einsum(
            "lkij,lkjp->lip",
            near_tiles,
            jnp.take(window_vec, near_local, axis=0),
            preferred_element_type=jnp.float32,
        )
        image = (near_part + far_part).reshape(-1, probes) + noise_var[:, None] * iterate
        iterate = iterate + relax_step * (right_side - image)
    return iterate


def solution(mesh):
    return jax.shard_map(
        per_device,
        mesh=mesh,
        in_specs=(
            P(("sub", "grp"), None),
            P(("sub", "grp")),
            P(("sub", "grp"), None, None, None),
            P(("sub", "grp"), None),
            P(("sub", "grp"), None, None),
            P(("sub", "grp"), None, None),
            P(("sub", "grp"), None, None, None),
            P(("sub", "grp"), None),
            P(("sub", "grp"), None, None),
            P(("sub", "grp"), None, None, None),
            P(("sub", "grp"), None),
            P("grp", None, None, None),
            P("grp", None),
        ),
        out_specs=P(("sub", "grp"), None),
        check_vma=False,
    )
```

profile of v0, /device:TPU:0, one launch (start us, length us, event | category | flops | bytes accessed | tf_op | source)
XLA Modules:
  0.0 426.6 jit_solution(17247988872576783730)
XLA Ops:
  3.3 6.0 %collective-permute-start.3 = (bf16[6,64,128]{2,1,0:T(8,128)(2,1)S(1)}, bf16[6,64,128]{2,1,0:T(8,128)(2,1)S(1)}, u32[]{:S(2)}, u32[]{:S(2)}) collective-permute-start(bf16[6,64,128]{2,1,0:T(8,128)(2,1)S(1)} %get-tuple-element.32), channel_id=1, source_target_pairs={{0,31},{1,0},{2,1},{3,2},{4,3},{5,4},{6,5},{7,6},{8,7},{9,8},{10,9... | collective-permute-start | bytes 294920 | tf_op jit(solution)/shard_map/ppermute | solution.py:16
  11.6 30.6 %all-gather.1 = bf16[512,128]{1,0:T(8,128)(2,1)S(1)} all-gather(bf16[64,128]{1,0:T(8,128)(2,1)S(1)} %fusion.60), channel_id=3, replica_groups=mesh['sub'=8,'grp'=4] {'sub'}, dimensions={0}, use_global_device_ids=true | all-gather | bytes 147456 | tf_op jit(solution)/shard_map/all_gather | solution.py:68
  42.2 5.2 %all-gather.2 = bf16[256,128]{1,0:T(8,128)(2,1)S(1)} all-gather(bf16[64,128]{1,0:T(8,128)(2,1)S(1)} %reduce_sum.48), channel_id=4, replica_groups=mesh['sub'=8,'grp'=4] {'grp'}, dimensions={0}, use_global_device_ids=true | all-gather | bytes 81920 | tf_op jit(solution)/shard_map/all_gather | solution.py:75
  47.4 30.5 %all-gather = bf16[512,128]{1,0:T(8,128)(2,1)S(1)} all-gather(bf16[64,128]{1,0:T(8,128)(2,1)S(1)} %bitcast.356), channel_id=2, replica_groups=mesh['sub'=8,'grp'=4] {'sub'}, dimensions={0}, use_global_device_ids=true | all-gather | bytes 147456 | tf_op jit(solution)/shard_map/all_gather | solution.py:67
  82.9 2.7 gather_fusion
  85.6 4.6 %copy.26 = bf16[8,6,256,128]{2,3,1,0:T(8,128)(2,1)} copy(bf16[8,6,256,128]{3,2,1,0:T(8,128)(2,1)} %bitcast.321) | data formatting | bytes 6291456 | tf_op jit(solution)/shard_map/jit(_take)/gather | solution.py:111
  90.2 5.9 %fusion.20 = f32[8,128,256]{2,1,0:T(8,128)S(1)} fusion(bf16[8,6,256,256]{3,2,1,0:T(8,128)(2,1)} %param.23, bf16[8,6,256,128]{2,3,1,0:T(8,128)(2,1)} %copy.26, pred[8,6]{1,0:T(8,128)(4,1)S(1)} %get-tuple-element.15), kind=kOutput, calls=%fused_computation.40 | convolution fusion | flops 806879232 | bytes 10485808 | tf_op jit(solution)/shard_map/lkij,lkjp->lip/dot_general | solution.py:108
  101.9 30.5 %all-gather.4 = bf16[512,128]{1,0:T(8,128)(2,1)S(1)} all-gather(bf16[64,128]{1,0:T(8,128)(2,1)S(1)} %fusion.61), channel_id=6, replica_groups=mesh['sub'=8,'grp'=4] {'sub'}, dimensions={0}, use_global_device_ids=true | all-gather | bytes 147456 | tf_op jit(solution)/shard_map/all_gather | solution.py:68
  132.4 5.2 %all-gather.5 = bf16[256,128]{1,0:T(8,128)(2,1)S(1)} all-gather(bf16[64,128]{1,0:T(8,128)(2,1)S(1)} %reduce_sum.49), channel_id=7, replica_groups=mesh['sub'=8,'grp'=4] {'grp'}, dimensions={0}, use_global_device_ids=true | all-gather | bytes 81920 | tf_op jit(solution)/shard_map/all_gather | solution.py:75
  138.3 30.5 %all-gather.3 = bf16[512,128]{1,0:T(8,128)(2,1)S(1)} all-gather(bf16[64,128]{1,0:T(8,128)(2,1)S(1)} %bitcast.354), channel_id=5, replica_groups=mesh['sub'=8,'grp'=4] {'sub'}, dimensions={0}, use_global_device_ids=true | all-gather | bytes 147456 | tf_op jit(solution)/shard_map/all_gather | solution.py:67
  169.7 5.3 %collective-permute-start.7 = (bf16[6,64,128]{2,1,0:T(8,128)(2,1)}, bf16[6,64,128]{2,1,0:T(8,128)(2,1)S(1)}, u32[]{:S(2)}, u32[]{:S(2)}) collective-permute-start(bf16[6,64,128]{2,1,0:T(8,128)(2,1)} %get-tuple-element.30), channel_id=1, source_target_pairs={{0,31},{1,0},{2,1},{3,2},{4,3},{5,4},{6,5},{7,6},{8,7},{9,8},{10,9... | collective-permute-start | bytes 294920 | tf_op jit(solution)/shard_map/ppermute | solution.py:16
  181.7 4.5 %collective-permute-done.4 = bf16[6,256,128]{2,1,0:T(8,128)(2,1)} collective-permute-done((bf16[6,256,128]{2,1,0:T(8,128)(2,1)}, bf16[6,256,128]{2,1,0:T(8,128)(2,1)}, u32[]{:S(2)}, u32[]{:S(2)}) %collective-permute-start.4) | collective-permute-done | bytes 393248 | tf_op jit(solution)/shard_map/ppermute | solution.py:16
  190.3 4.6 %copy.30 = bf16[8,6,256,128]{2,3,1,0:T(8,128)(2,1)} copy(bf16[8,6,256,128]{3,2,1,0:T(8,128)(2,1)} %bitcast.322) | data formatting | bytes 6291456 | tf_op jit(solution)/shard_map/jit(_take)/gather | solution.py:111
  194.9 6.9 %fusion.23 = f32[8,128,256]{2,1,0:T(8,128)} fusion(bf16[8,6,256,256]{3,2,1,0:T(8,128)(2,1)} %param.23, bf16[8,6,256,128]{2,3,1,0:T(8,128)(2,1)} %copy.30, pred[8,6]{1,0:T(8,128)(4,1)S(1)} %get-tuple-element.15), kind=kOutput, calls=%fused_computation.41 | convolution fusion | flops 806879232 | bytes 10485808 | tf_op jit(solution)/shard_map/lkij,lkjp->lip/dot_general | solution.py:108
  201.9 2.8 fusion.18
  211.6 30.5 %all-gather.7 = bf16[512,128]{1,0:T(8,128)(2,1)S(1)} all-gather(bf16[64,128]{1,0:T(8,128)(2,1)S(1)} %fusion.62), channel_id=9, replica_groups=mesh['sub'=8,'grp'=4] {'sub'}, dimensions={0}, use_global_device_ids=true | all-gather | bytes 147456 | tf_op jit(solution)/shard_map/all_gather | solution.py:68
  242.2 5.4 %all-gather.8 = bf16[256,128]{1,0:T(8,128)(2,1)S(1)} all-gather(bf16[64,128]{1,0:T(8,128)(2,1)S(1)} %reduce_sum.50), channel_id=10, replica_groups=mesh['sub'=8,'grp'=4] {'grp'}, dimensions={0}, use_global_device_ids=true | all-gather | bytes 81920 | tf_op jit(solution)/shard_map/all_gather | solution.py:75
  248.2 30.5 %all-gather.6 = bf16[512,128]{1,0:T(8,128)(2,1)S(1)} all-gather(bf16[64,128]{1,0:T(8,128)(2,1)S(1)} %bitcast.355), channel_id=8, replica_groups=mesh['sub'=8,'grp'=4] {'sub'}, dimensions={0}, use_global_device_ids=true | all-gather | bytes 147456 | tf_op jit(solution)/shard_map/all_gather | solution.py:67
  279.6 5.3 %collective-permute-start.11 = (bf16[6,64,128]{2,1,0:T(8,128)(2,1)S(1)}, bf16[6,64,128]{2,1,0:T(8,128)(2,1)S(1)}, u32[]{:S(2)}, u32[]{:S(2)}) collective-permute-start(bf16[6,64,128]{2,1,0:T(8,128)(2,1)S(1)} %get-tuple-element.28), channel_id=1, source_target_pairs={{0,31},{1,0},{2,1},{3,2},{4,3},{5,4},{6,5},{7,6},{8,7},{9,8},{10,9... | collective-permute-start | bytes 294920 | tf_op jit(solution)/shard_map/ppermute | solution.py:16
  291.4 4.7 %collective-permute-done.8 = bf16[6,256,128]{2,1,0:T(8,128)(2,1)} collective-permute-done((bf16[6,256,128]{2,1,0:T(8,128)(2,1)}, bf16[6,256,128]{2,1,0:T(8,128)(2,1)}, u32[]{:S(2)}, u32[]{:S(2)}) %collective-permute-start.8) | collective-permute-done | bytes 393248 | tf_op jit(solution)/shard_map/ppermute | solution.py:16
  300.2 4.6 %copy.34 = bf16[8,6,256,128]{2,3,1,0:T(8,128)(2,1)} copy(bf16[8,6,256,128]{3,2,1,0:T(8,128)(2,1)} %bitcast.323) | data formatting | bytes 6291456 | tf_op jit(solution)/shard_map/jit(_take)/gather | solution.py:111
  304.9 5.9 %fusion.26 = f32[8,128,256]{2,1,0:T(8,128)S(1)} fusion(bf16[8,6,256,256]{3,2,1,0:T(8,128)(2,1)} %param.23, bf16[8,6,256,128]{2,3,1,0:T(8,128)(2,1)} %copy.34, pred[8,6]{1,0:T(8,128)(4,1)S(1)} %get-tuple-element.15), kind=kOutput, calls=%fused_computation.42 | convolution fusion | flops 806879232 | bytes 10485808 | tf_op jit(solution)/shard_map/lkij,lkjp->lip/dot_general | solution.py:108
  318.1 30.6 %all-gather.10 = bf16[512,128]{1,0:T(8,128)(2,1)S(1)} all-gather(bf16[64,128]{1,0:T(8,128)(2,1)S(1)} %fusion.63), channel_id=12, replica_groups=mesh['sub'=8,'grp'=4] {'sub'}, dimensions={0}, use_global_device_ids=true | all-gather | bytes 147456 | tf_op jit(solution)/shard_map/all_gather | solution.py:68
  348.7 5.2 %all-gather.11 = bf16[256,128]{1,0:T(8,128)(2,1)S(1)} all-gather(bf16[64,128]{1,0:T(8,128)(2,1)S(1)} %reduce_sum.51), channel_id=13, replica_groups=mesh['sub'=8,'grp'=4] {'grp'}, dimensions={0}, use_global_device_ids=true | all-gather | bytes 81920 | tf_op jit(solution)/shard_map/all_gather | solution.py:75
  354.5 30.5 %all-gather.9 = bf16[512,128]{1,0:T(8,128)(2,1)S(1)} all-gather(bf16[64,128]{1,0:T(8,128)(2,1)S(1)} %bitcast.353), channel_id=11, replica_groups=mesh['sub'=8,'grp'=4] {'sub'}, dimensions={0}, use_global_device_ids=true | all-gather | bytes 147456 | tf_op jit(solution)/shard_map/all_gather | solution.py:67
  386.0 5.3 %collective-permute-start.15 = (bf16[6,64,128]{2,1,0:T(8,128)(2,1)}, bf16[6,64,128]{2,1,0:T(8,128)(2,1)S(1)}, u32[]{:S(2)}, u32[]{:S(2)}) collective-permute-start(bf16[6,64,128]{2,1,0:T(8,128)(2,1)} %get-tuple-element.26), channel_id=1, source_target_pairs={{0,31},{1,0},{2,1},{3,2},{4,3},{5,4},{6,5},{7,6},{8,7},{9,8},{10,9... | collective-permute-start | bytes 294920 | tf_op jit(solution)/shard_map/ppermute | solution.py:16
  397.9 4.5 %collective-permute-done.12 = bf16[6,256,128]{2,1,0:T(8,128)(2,1)} collective-permute-done((bf16[6,256,128]{2,1,0:T(8,128)(2,1)}, bf16[6,256,128]{2,1,0:T(8,128)(2,1)}, u32[]{:S(2)}, u32[]{:S(2)}) %collective-permute-start.12) | collective-permute-done | bytes 393248 | tf_op jit(solution)/shard_map/ppermute | solution.py:16
  403.9 2.7 gather_fusion.12
  406.6 4.7 %copy.38 = bf16[8,6,256,128]{2,3,1,0:T(8,128)(2,1)} copy(bf16[8,6,256,128]{3,2,1,0:T(8,128)(2,1)} %bitcast.320) | data formatting | bytes 6291456 | tf_op jit(solution)/shard_map/jit(_take)/gather | solution.py:111
  411.3 6.9 %fusion.29 = f32[8,128,256]{2,1,0:T(8,128)} fusion(bf16[8,6,256,256]{3,2,1,0:T(8,128)(2,1)} %param.23, bf16[8,6,256,128]{2,3,1,0:T(8,128)(2,1)} %copy.38, pred[8,6]{1,0:T(8,128)(4,1)S(1)} %get-tuple-element.15), kind=kOutput, calls=%fused_computation.43 | convolution fusion | flops 806879232 | bytes 10485808 | tf_op jit(solution)/shard_map/lkij,lkjp->lip/dot_general | solution.py:108
  418.2 2.9 fusion.16
  423.6 3.0 fusion.66
  (155 shorter events, 66.6 us)
Async XLA Ops:
  0.0 80.5 %copy-start = (bf16[8,4,64,64]{3,2,1,0:T(8,128)(2,1)S(1)}, bf16[8,4,64,64]{3,2,1,0:T(8,128)(2,1)}, u32[]{:S(2)}) copy-start(bf16[8,4,64,64]{3,2,1,0:T(8,128)(2,1)} %param.27) | copy-start | bytes 786436
  0.0 10.7 %copy-start.21 = (s32[1,3]{1,0:T(1,128)S(1)}, s32[1,3]{1,0:T(1,128)}, u32[]{:S(2)}) copy-start(s32[1,3]{1,0:T(1,128)} %param.33) | copy-start | bytes 40
  0.0 10.8 %copy-start.22 = (s32[1,4]{1,0:T(1,128)S(1)}, s32[1,4]{1,0:T(1,128)}, u32[]{:S(2)}) copy-start(s32[1,4]{1,0:T(1,128)} %param.31) | copy-start | bytes 52
  0.0 10.8 %copy-start.20 = (s32[8,4]{0,1:T(4,128)S(1)}, s32[8,4]{0,1:T(4,128)}, u32[]{:S(2)}) copy-start(s32[8,4]{0,1:T(4,128)} %param.28) | copy-start | bytes 388
  0.0 11.1 %copy-start.19 = (s32[8,6]{1,0:T(8,128)S(1)}, s32[8,6]{1,0:T(8,128)}, u32[]{:S(2)}) copy-start(s32[8,6]{1,0:T(8,128)} %param.24) | copy-start | bytes 580
  0.0 11.2 %copy-start.17 = (f32[2048]{0:T(1024)S(1)}, f32[2048]{0:T(1024)}, u32[]{:S(2)}) copy-start(f32[2048]{0:T(1024)} %param.22) | copy-start | bytes 24580
  0.0 11.2 %copy-start.10 = (bf16[8,64,64]{2,1,0:T(8,128)(2,1)S(1)}, bf16[8,64,64]{2,1,0:T(8,128)(2,1)}, u32[]{:S(2)}) copy-start(bf16[8,64,64]{2,1,0:T(8,128)(2,1)} %param.26) | copy-start | bytes 196612
  0.0 11.4 %copy-start.12 = (bf16[1,64,64]{2,1,0:T(8,128)(2,1)S(1)}, bf16[1,64,64]{2,1,0:T(8,128)(2,1)}, u32[]{:S(2)}) copy-start(bf16[1,64,64]{2,1,0:T(8,128)(2,1)} %param.29) | copy-start | bytes 24580
  0.1 79.0 %copy-start.11 = (bf16[1,4,64,64]{3,2,1,0:T(8,128)(2,1)S(1)}, bf16[1,4,64,64]{3,2,1,0:T(8,128)(2,1)}, u32[]{:S(2)}) copy-start(bf16[1,4,64,64]{3,2,1,0:T(8,128)(2,1)} %param.30) | copy-start | bytes 98308
  0.1 79.3 %copy-start.13 = (bf16[1,3,64,64]{3,2,1,0:T(8,128)(2,1)S(1)}, bf16[1,3,64,64]{3,2,1,0:T(8,128)(2,1)}, u32[]{:S(2)}) copy-start(bf16[1,3,64,64]{3,2,1,0:T(8,128)(2,1)} %param.32) | copy-start | bytes 73732
  2.7 77.1 %collective-permute-start.2 = (bf16[6,64,128]{2,1,0:T(8,128)(2,1)S(1)}, bf16[6,64,128]{2,1,0:T(8,128)(2,1)S(1)}, u32[]{:S(2)}, u32[]{:S(2)}) collective-permute-start(bf16[6,64,128]{2,1,0:T(8,128)(2,1)S(1)} %get-tuple-element.31), channel_id=1, source_target_pairs={{0,1},{1,2},{2,3},{3,4},{4,5},{5,6},{6,7},{7,8},{8,9},{9,10},{10,1... | collective-permute-start | bytes 294920 | tf_op jit(solution)/shard_map/ppermute | solution.py:16
  3.3 76.5 %collective-permute-start.3 = (bf16[6,64,128]{2,1,0:T(8,128)(2,1)S(1)}, bf16[6,64,128]{2,1,0:T(8,128)(2,1)S(1)}, u32[]{:S(2)}, u32[]{:S(2)}) collective-permute-start(bf16[6,64,128]{2,1,0:T(8,128)(2,1)S(1)} %get-tuple-element.32), channel_id=1, source_target_pairs={{0,31},{1,0},{2,1},{3,2},{4,3},{5,4},{6,5},{7,6},{8,7},{9,8},{10,9... | collective-permute-start | bytes 294920 | tf_op jit(solution)/shard_map/ppermute | solution.py:16
  10.0 70.8 %collective-permute-start.1 = (bf16[6,256,128]{2,1,0:T(8,128)(2,1)}, bf16[6,256,128]{2,1,0:T(8,128)(2,1)S(1)}, u32[]{:S(2)}, u32[]{:S(2)}) collective-permute-start(bf16[6,256,128]{2,1,0:T(8,128)(2,1)} %bitcast.6), channel_id=1, source_target_pairs={{0,31},{1,0},{2,1},{3,2},{4,3},{5,4},{6,5},{7,6},{8,7},{9,8},{10,9... | collective-permute-start | bytes 1179656 | tf_op jit(solution)/shard_map/ppermute | solution.py:16
  10.7 70.9 %collective-permute-start = (bf16[6,256,128]{2,1,0:T(8,128)(2,1)S(1)}, bf16[6,256,128]{2,1,0:T(8,128)(2,1)}, u32[]{:S(2)}, u32[]{:S(2)}) collective-permute-start(bf16[6,256,128]{2,1,0:T(8,128)(2,1)S(1)} %bitcast.340), channel_id=1, source_target_pairs={{0,1},{1,2},{2,3},{3,4},{4,5},{5,6},{6,7},{7,8},{8,9},{9,10},{10,1... | collective-permute-start | bytes 1179656 | tf_op jit(solution)/shard_map/ppermute | solution.py:16
  10.9 277.1 %copy-start.23 = (pred[8,4]{1,0:T(8,128)(4,1)}, pred[8,4]{1,0:T(8,128)(4,1)S(1)}, u32[]{:S(2)}) copy-start(pred[8,4]{1,0:T(8,128)(4,1)S(1)} %copy.27) | copy-start | bytes 100
  90.2 6.0 %copy-start.2 = (bf16[8,64,256]{2,1,0:T(8,128)(2,1)S(1)}, bf16[8,64,256]{2,1,0:T(8,128)(2,1)}, u32[]{:S(2)}) copy-start(bf16[8,64,256]{2,1,0:T(8,128)(2,1)} %param.25) | copy-start | bytes 786436
  99.3 39.0 %copy-start.8 = (f32[8,256,128]{2,1,0:T(8,128)}, f32[8,256,128]{2,1,0:T(8,128)S(1)}, u32[]{:S(2)}) copy-start(f32[8,256,128]{2,1,0:T(8,128)S(1)} %copy.29) | copy-start | bytes 3145732
  169.7 8.0 %collective-permute-start.6 = (bf16[6,64,128]{2,1,0:T(8,128)(2,1)}, bf16[6,64,128]{2,1,0:T(8,128)(2,1)S(1)}, u32[]{:S(2)}, u32[]{:S(2)}) collective-permute-start(bf16[6,64,128]{2,1,0:T(8,128)(2,1)} %get-tuple-element.29), channel_id=1, source_target_pairs={{0,1},{1,2},{2,3},{3,4},{4,5},{5,6},{6,7},{7,8},{8,9},{9,10},{10,1... | collective-permute-start | bytes 294920 | tf_op jit(solution)/shard_map/ppermute | solution.py:16
  169.7 7.9 %collective-permute-start.7 = (bf16[6,64,128]{2,1,0:T(8,128)(2,1)}, bf16[6,64,128]{2,1,0:T(8,128)(2,1)S(1)}, u32[]{:S(2)}, u32[]{:S(2)}) collective-permute-start(bf16[6,64,128]{2,1,0:T(8,128)(2,1)} %get-tuple-element.30), channel_id=1, source_target_pairs={{0,31},{1,0},{2,1},{3,2},{4,3},{5,4},{6,5},{7,6},{8,7},{9,8},{10,9... | collective-permute-start | bytes 294920 | tf_op jit(solution)/shard_map/ppermute | solution.py:16
  175.0 6.7 %collective-permute-start.5 = (bf16[6,256,128]{2,1,0:T(8,128)(2,1)}, bf16[6,256,128]{2,1,0:T(8,128)(2,1)}, u32[]{:S(2)}, u32[]{:S(2)}) collective-permute-start(bf16[6,256,128]{2,1,0:T(8,128)(2,1)} %bitcast.344), channel_id=1, source_target_pairs={{0,31},{1,0},{2,1},{3,2},{4,3},{5,4},{6,5},{7,6},{8,7},{9,8},{10,9... | collective-permute-start | bytes 1179656 | tf_op jit(solution)/shard_map/ppermute | solution.py:16
  175.1 11.1 %collective-permute-start.4 = (bf16[6,256,128]{2,1,0:T(8,128)(2,1)}, bf16[6,256,128]{2,1,0:T(8,128)(2,1)}, u32[]{:S(2)}, u32[]{:S(2)}) collective-permute-start(bf16[6,256,128]{2,1,0:T(8,128)(2,1)} %bitcast.343), channel_id=1, source_target_pairs={{0,1},{1,2},{2,3},{3,4},{4,5},{5,6},{6,7},{7,8},{8,9},{9,10},{10,1... | collective-permute-start | bytes 1179656 | tf_op jit(solution)/shard_map/ppermute | solution.py:16
  194.9 6.9 %copy-start.15 = (f32[8,64,128]{2,1,0:T(8,128)S(1)}, f32[8,64,128]{2,1,0:T(8,128)}, u32[]{:S(2)}) copy-start(f32[8,64,128]{2,1,0:T(8,128)} %convolution_bitcast_fusion.2) | copy-start | bytes 786436
  279.6 7.8 %collective-permute-start.10 = (bf16[6,64,128]{2,1,0:T(8,128)(2,1)S(1)}, bf16[6,64,128]{2,1,0:T(8,128)(2,1)S(1)}, u32[]{:S(2)}, u32[]{:S(2)}) collective-permute-start(bf16[6,64,128]{2,1,0:T(8,128)(2,1)S(1)} %get-tuple-element.27), channel_id=1, source_target_pairs={{0,1},{1,2},{2,3},{3,4},{4,5},{5,6},{6,7},{7,8},{8,9},{9,10},{10,1... | collective-permute-start | bytes 294920 | tf_op jit(solution)/shard_map/ppermute | solution.py:16
  279.6 7.7 %collective-permute-start.11 = (bf16[6,64,128]{2,1,0:T(8,128)(2,1)S(1)}, bf16[6,64,128]{2,1,0:T(8,128)(2,1)S(1)}, u32[]{:S(2)}, u32[]{:S(2)}) collective-permute-start(bf16[6,64,128]{2,1,0:T(8,128)(2,1)S(1)} %get-tuple-element.28), channel_id=1, source_target_pairs={{0,31},{1,0},{2,1},{3,2},{4,3},{5,4},{6,5},{7,6},{8,7},{9,8},{10,9... | collective-permute-start | bytes 294920 | tf_op jit(solution)/shard_map/ppermute | solution.py:16
  285.0 6.5 %collective-permute-start.9 = (bf16[6,256,128]{2,1,0:T(8,128)(2,1)}, bf16[6,256,128]{2,1,0:T(8,128)(2,1)}, u32[]{:S(2)}, u32[]{:S(2)}) collective-permute-start(bf16[6,256,128]{2,1,0:T(8,128)(2,1)} %bitcast.57), channel_id=1, source_target_pairs={{0,31},{1,0},{2,1},{3,2},{4,3},{5,4},{6,5},{7,6},{8,7},{9,8},{10,9... | collective-permute-start | bytes 1179656 | tf_op jit(solution)/shard_map/ppermute | solution.py:16
  285.0 11.1 %collective-permute-start.8 = (bf16[6,256,128]{2,1,0:T(8,128)(2,1)}, bf16[6,256,128]{2,1,0:T(8,128)(2,1)}, u32[]{:S(2)}, u32[]{:S(2)}) collective-permute-start(bf16[6,256,128]{2,1,0:T(8,128)(2,1)} %bitcast.55), channel_id=1, source_target_pairs={{0,1},{1,2},{2,3},{3,4},{4,5},{5,6},{6,7},{7,8},{8,9},{9,10},{10,1... | collective-permute-start | bytes 1179656 | tf_op jit(solution)/shard_map/ppermute | solution.py:16
  304.8 5.9 %copy-start.16 = (f32[8,64,128]{2,1,0:T(8,128)S(1)}, f32[8,64,128]{2,1,0:T(8,128)}, u32[]{:S(2)}) copy-start(f32[8,64,128]{2,1,0:T(8,128)} %convolution_bitcast_fusion.1) | copy-start | bytes 786436
  385.9 8.0 %collective-permute-start.14 = (bf16[6,64,128]{2,1,0:T(8,128)(2,1)}, bf16[6,64,128]{2,1,0:T(8,128)(2,1)S(1)}, u32[]{:S(2)}, u32[]{:S(2)}) collective-permute-start(bf16[6,64,128]{2,1,0:T(8,128)(2,1)} %get-tuple-element.25), channel_id=1, source_target_pairs={{0,1},{1,2},{2,3},{3,4},{4,5},{5,6},{6,7},{7,8},{8,9},{9,10},{10,1... | collective-permute-start | bytes 294920 | tf_op jit(solution)/shard_map/ppermute | solution.py:16
  386.0 7.9 %collective-permute-start.15 = (bf16[6,64,128]{2,1,0:T(8,128)(2,1)}, bf16[6,64,128]{2,1,0:T(8,128)(2,1)S(1)}, u32[]{:S(2)}, u32[]{:S(2)}) collective-permute-start(bf16[6,64,128]{2,1,0:T(8,128)(2,1)} %get-tuple-element.26), channel_id=1, source_target_pairs={{0,31},{1,0},{2,1},{3,2},{4,3},{5,4},{6,5},{7,6},{8,7},{9,8},{10,9... | collective-permute-start | bytes 294920 | tf_op jit(solution)/shard_map/ppermute | solution.py:16
  391.3 6.7 %collective-permute-start.13 = (bf16[6,256,128]{2,1,0:T(8,128)(2,1)}, bf16[6,256,128]{2,1,0:T(8,128)(2,1)}, u32[]{:S(2)}, u32[]{:S(2)}) collective-permute-start(bf16[6,256,128]{2,1,0:T(8,128)(2,1)} %bitcast.342), channel_id=1, source_target_pairs={{0,31},{1,0},{2,1},{3,2},{4,3},{5,4},{6,5},{7,6},{8,7},{9,8},{10,9... | collective-permute-start | bytes 1179656 | tf_op jit(solution)/shard_map/ppermute | solution.py:16
  391.3 11.1 %collective-permute-start.12 = (bf16[6,256,128]{2,1,0:T(8,128)(2,1)}, bf16[6,256,128]{2,1,0:T(8,128)(2,1)}, u32[]{:S(2)}, u32[]{:S(2)}) collective-permute-start(bf16[6,256,128]{2,1,0:T(8,128)(2,1)} %bitcast.341), channel_id=1, source_target_pairs={{0,1},{1,2},{2,3},{3,4},{4,5},{5,6},{6,7},{7,8},{8,9},{9,10},{10,1... | collective-permute-start | bytes 1179656 | tf_op jit(solution)/shard_map/ppermute | solution.py:16
  411.3 6.9 %copy-start.18 = (bf16[128,64,1]{1,0,2:T(8,128)(2,1)S(1)}, bf16[128,64,1]{1,0,2:T(8,128)(2,1)}, u32[]{:S(2)}) copy-start(bf16[128,64,1]{1,0,2:T(8,128)(2,1)} %fusion.52) | copy-start | bytes 49156
  (8 other events, 21.9 us)
where the time goes:
time: 428 us; the launch traced here: 427 us
  blocking collectives  265 us (62%)
  local copies, waits for them, and re-layouts  51.3 us (12%)
  matrix products  44.5 us (10%)
  starting transfers between devices  24.9 us (6%)
  waiting for transfers between devices  24.9 us (6%)
  other arithmetic  15.1 us (4%)
    all_gather x4, blocking collectives, per_device(): group_lifted = lax.all_gather(lifted[None], 'sub', axis=0, tiled=True)  122 us
    all_gather x4, blocking collectives, per_device(): group_coef = lax.all_gather(dev_coef[None], 'sub', axis=0, tiled=True)  122 us
    gather x8, local copies, waits for them, and re-layouts, per_device(): jnp.take(window_vec, near_local, axis=0)  29.4 us
    dot_general x4, matrix products, per_device(): jnp.einsum('lkij,lkjp->lip', near_tiles, jnp.take(window_vec, near_local,...  25.7 us
    ppermute x16, starting transfers between devices, from_behind(): return lax.ppermute(value, axis, pairs)  24.9 us
    ppermute x16, waiting for transfers between devices, from_behind(): return lax.ppermute(value, axis, pairs)  24.9 us
    all_gather x4, blocking collectives, per_device(): mid_coef = lax.all_gather(own_mids, 'grp', axis=0, tiled=True)  21.2 us
    dot_general x4, matrix products, per_device(): jnp.einsum('lrj,lrp->ljp', leaf_basis, leaf_field, preferred_element_type...  8.77 us
  transfers between devices with their start and end apart: 16, of which 9 were waited for; matrix products, arithmetic and copies ran while one was open for 3% of the time, Pallas kernels for 0%

commit v1 on v0

v1 whole, which is shorter than its diff:
```python
import functools

import jax
import jax.numpy as jnp
from jax import lax
from jax.experimental import pallas as pl
from jax.experimental.pallas import tpu as pltpu
from jax.sharding import PartitionSpec as P

SPAN = 6
ITERS = 4
MID_DEVS = 8
MESH = pl.DeviceIdType.MESH


relax_step = 0.3


def dot(a, b):
    return jnp.dot(a, b, preferred_element_type=jnp.float32)


def flip(a):
    return a.astype(jnp.float32).T.astype(jnp.bfloat16)


def kernel(
    groups,
    group_devs,
    near_ref,
    far_ref,
    fdev_ref,
    fmid_ref,
    rhs_ref,
    noise_ref,
    basis_ref,
    lt_ref,
    lc_ref,
    dt_ref,
    dc_ref,
    mc_ref,
    tiles_hbm,
    x_ref,
    tiles,
    basis_t,
    lt_t,
    dt_t,
    cwin,
    nbasis,
    dt_all,
    *rest,
):
    wins, rest = rest[:ITERS], rest[ITERS:]
    gaths, rest = rest[:ITERS], rest[ITERS:]
    mids, rest = rest[:ITERS], rest[ITERS:]
    (
        tile_sem,
        halo_send,
        halo_recv,
        nb_send,
        nb_recv,
        dt_send,
        dt_recv,
        g_send,
        g_recv,
        m_send,
        m_recv,
    ) = rest
    leaves = rhs_ref.shape[0]
    near = near_ref.shape[1]
    nfar = far_ref.shape[1]
    nfdev = fdev_ref.shape[1]
    nfmid = fmid_ref.shape[1]
    mid_grp = group_devs // MID_DEVS
    count = groups * group_devs
    sub = lax.axis_index("sub")
    grp = lax.axis_index("grp")
    me = sub * groups + grp
    nxt = lax.rem(me + 1, count)
    prv = lax.rem(me + count - 1, count)
    next_id = (nxt // groups, lax.rem(nxt, groups))
    prev_id = (prv // groups, lax.rem(prv, groups))

    def sub_peer(j):
        return lax.rem(sub + j, group_devs)

    def grp_peer(j):
        return lax.rem(grp + j, groups)

    def tile_copy(l):
        return pltpu.make_async_copy(tiles_hbm.at[l], tiles.at[l], tile_sem.at[l])

    for l in range(leaves):
        tile_copy(l).start()

    def remote(src, dst, send, recv, device):
        return pltpu.make_async_remote_copy(
            src_ref=src,
            dst_ref=dst,
            send_sem=send,
            recv_sem=recv,
            device_id=device,
            device_id_type=MESH,
        )

    def to_prev(it, l):
        return remote(
            wins[it].at[SPAN + l],
            wins[it].at[SPAN + leaves + l],
            halo_send.at[it, 0, l],
            halo_recv.at[it, 0, l],
            prev_id,
        )

    def to_next(it, h):
        return remote(
            wins[it].at[leaves + h],
            wins[it].at[h],
            halo_send.at[it, 1, h],
            halo_recv.at[it, 1, h],
            next_id,
        )

    def basis_copy(side):
        if side == 0:
            src, dst, device = basis_ref.at[pl.ds(0, SPAN)], nbasis.at[pl.ds(SPAN, SPAN)], prev_id
        else:
            src, dst, device = (
                basis_ref.at[pl.ds(leaves - SPAN, SPAN)],
                nbasis.at[pl.ds(0, SPAN)],
                next_id,
            )
        return remote(src, dst, nb_send.at[side], nb_recv.at[side], device)

    def dt_copy(j, owner):
        return remote(
            dt_ref.at[0], dt_all.at[owner], dt_send.at[j], dt_recv.at[j], (sub_peer(j), grp)
        )

    def gath_copy(it, j, owner):
        block = gaths[it].at[owner]
        return remote(block, block, g_send.at[it, j], g_recv.at[it, j], (sub_peer(j), grp))

    def mid_copy(it, j, owner):
        block = mids[it].at[pl.ds(owner * mid_grp, mid_grp)]
        return remote(block, block, m_send.at[it, j], m_recv.at[it, j], (sub, grp_peer(j)))

    barrier = pltpu.get_barrier_semaphore()
    for device in (prev_id, next_id):
        pl.semaphore_signal(barrier, inc=1, device_id=device, device_id_type=MESH)
    for j in range(1, group_devs):
        pl.semaphore_signal(barrier, inc=1, device_id=(sub_peer(j), grp), device_id_type=MESH)
    for j in range(1, groups):
        pl.semaphore_signal(barrier, inc=1, device_id=(sub, grp_peer(j)), device_id_type=MESH)

    for l in range(leaves):
        start = relax_step * rhs_ref[l]
        x_ref[l] = start
        wins[0][SPAN + l] = start.astype(jnp.bfloat16)
    pl.semaphore_wait(barrier, 2 + (group_devs - 1) + (groups - 1))

    for j in range(1, group_devs):
        dt_copy(j, sub).start()
    for l in range(SPAN):
        to_prev(0, l).start()
        to_next(0, l).start()
    basis_copy(0).start()
    basis_copy(1).start()

    dt_all[sub] = dt_ref[0]
    dt_t[...] = flip(dt_ref[0])
    for l in range(leaves):
        basis_t[l] = flip(basis_ref[l])
        lt_t[l] = flip(lt_ref[l])

    for it in range(ITERS):
        win, gath, mid = wins[it], gaths[it], mids[it]
        total = None
        for l in range(leaves):
            coef = dot(basis_ref[l], win[SPAN + l]).astype(jnp.bfloat16)
            cwin[SPAN + l] = coef
            term = dot(lt_ref[l], coef)
            total = term if total is None else total + term
        gath[sub] = total.astype(jnp.bfloat16)
        for j in range(1, group_devs):
            gath_copy(it, j, sub).start()

        for j in range(1, group_devs):
            owner = lax.rem(sub + group_devs - j, group_devs)
            if it == 0:
                dt_copy(j, owner).wait_recv()
            gath_copy(it, j, owner).wait_recv()
        for m in range(mid_grp):
            lifted = None
            for s in range(MID_DEVS):
                place = m * MID_DEVS + s
                term = dot(dt_all[place], gath[place]).astype(jnp.bfloat16).astype(jnp.float32)
                lifted = term if lifted is None else lifted + term
            mid[grp * mid_grp + m] = lifted.astype(jnp.bfloat16)
        for j in range(1, groups):
            mid_copy(it, j, grp).start()

        dev_total = None
        for k in range(nfdev):
            term = dot(dc_ref[0, k], gath[fdev_ref[0, k]])
            dev_total = term if dev_total is None else dev_total + term
        for j in range(1, groups):
            owner = lax.rem(grp + groups - j, groups)
            mid_copy(it, j, owner).wait_recv()
        own_mid = sub // MID_DEVS
        field = None
        for k in range(nfmid):
            term = dot(mc_ref[own_mid, k], mid[fmid_ref[own_mid, k]])
            field = term if field is None else field + term
        dev_field = (dev_total + dot(dt_t[...], field.astype(jnp.bfloat16))).astype(jnp.bfloat16)

        if it == 0:
            basis_copy(0).wait_recv()
            basis_copy(1).wait_recv()
        for h in range(SPAN):
            to_prev(it, h).wait_recv()
            place = SPAN + leaves + h
            cwin[place] = dot(nbasis[SPAN + h], win[place]).astype(jnp.bfloat16)
            to_next(it, h).wait_recv()
            cwin[h] = dot(nbasis[h], win[h]).astype(jnp.bfloat16)

        def leaf_step(l, carry, it=it, win=win, dev_field=dev_field):
            if it == 0:
                tile_copy(l).wait()
            acc = dot(lt_t[l], dev_field)
            for k in range(nfar):
                acc = acc + dot(lc_ref[l, k], cwin[far_ref[l, k]])
            image = dot(basis_t[l], acc.astype(jnp.bfloat16))
            for k in range(near):
                image = image + dot(tiles[l, k], win[near_ref[l, k]])
            old = x_ref[l]
            image = image + noise_ref[l] * old
            new = old + relax_step * (rhs_ref[l] - image)
            x_ref[l] = new
            if it + 1 < ITERS:
                wins[it + 1][SPAN + l] = new.astype(jnp.bfloat16)

                @pl.when(l < SPAN)
                def _():
                    to_prev(it + 1, l).start()

                @pl.when(l >= leaves - SPAN)
                def _():
                    to_next(it + 1, l - (leaves - SPAN)).start()

            return carry

        lax.fori_loop(0, leaves, leaf_step, 0)

    for j in range(1, group_devs):
        dt_copy(j, sub).wait_send()
    basis_copy(0).wait_send()
    basis_copy(1).wait_send()
    for it in range(ITERS):
        for h in range(SPAN):
            to_prev(it, h).wait_send()
            to_next(it, h).wait_send()
        for j in range(1, group_devs):
            gath_copy(it, j, sub).wait_send()
        for j in range(1, groups):
            mid_copy(it, j, grp).wait_send()


def per_device(
    right_side,
    noise_var,
    near_tiles,
    near_index,
    leaf_basis,
    leaf_transfer,
    leaf_coupling,
    far_leaf,
    dev_transfer,
    dev_coupling,
    far_dev,
    mid_coupling,
    far_mid,
):
    leaves, near, size, _ = near_tiles.shape
    probes = right_side.shape[1]
    rank = leaf_basis.shape[1]
    groups = lax.axis_size("grp")
    group_devs = lax.axis_size("sub")
    total_leaves = leaves * groups * group_devs
    device = lax.axis_index("sub") * groups + lax.axis_index("grp")
    first_leaf = device * leaves
    near_local = jnp.mod(near_index - first_leaf + SPAN, total_leaves)
    far_local = jnp.mod(far_leaf - first_leaf + SPAN, total_leaves)
    far_within = far_dev // groups
    window = leaves + 2 * SPAN
    all_mids = groups * (group_devs // MID_DEVS)
    bf16 = jnp.bfloat16
    smem = pl.BlockSpec(memory_space=pltpu.SMEM)
    vmem = pl.BlockSpec(memory_space=pltpu.VMEM)
    dma = pltpu.SemaphoreType.DMA
    scratch = [
        pltpu.VMEM((leaves, near, size, size), bf16),
        pltpu.VMEM((leaves, size, rank), bf16),
        pltpu.VMEM((leaves, rank, rank), bf16),
        pltpu.VMEM((rank, rank), bf16),
        pltpu.VMEM((window, rank, probes), bf16),
        pltpu.VMEM((2 * SPAN, rank, size), bf16),
        pltpu.VMEM((group_devs, rank, rank), bf16),
    ]
    scratch += [pltpu.VMEM((window, size, probes), bf16)] * ITERS
    scratch += [pltpu.VMEM((group_devs, rank, probes), bf16)] * ITERS
    scratch += [pltpu.VMEM((all_mids, rank, probes), bf16)] * ITERS
    scratch += [
        dma((leaves,)),
        dma((ITERS, 2, SPAN)),
        dma((ITERS, 2, SPAN)),
        dma((2,)),
        dma((2,)),
        dma((group_devs,)),
        dma((group_devs,)),
        dma((ITERS, group_devs)),
        dma((ITERS, group_devs)),
        dma((ITERS, groups)),
        dma((ITERS, groups)),
    ]
    out = pl.pallas_call(
        functools.partial(kernel, groups, group_devs),
        out_shape=jax.ShapeDtypeStruct((leaves, size, probes), jnp.float32),
        in_specs=[smem] * 4 + [vmem] * 8 + [pl.BlockSpec(memory_space=pl.ANY)],
        out_specs=vmem,
        scratch_shapes=scratch,
        compiler_params=pltpu.CompilerParams(
            collective_id=0, has_side_effects=True, vmem_limit_bytes=48 * 1024 * 1024
        ),
    )(
        near_local,
        far_local,
        far_within,
        far_mid,
        right_side.reshape(leaves, size, probes),
        noise_var.reshape(leaves, size, 1),
        leaf_basis,
        leaf_transfer,
        leaf_coupling,
        dev_transfer,
        dev_coupling,
        mid_coupling,
        near_tiles,
    )
    return out.reshape(leaves * size, probes)


def solution(mesh):
    return jax.shard_map(
        per_device,
        mesh=mesh,
        in_specs=(
            P(("sub", "grp"), None),
            P(("sub", "grp")),
            P(("sub", "grp"), None, None, None),
            P(("sub", "grp"), None),
            P(("sub", "grp"), None, None),
            P(("sub", "grp"), None, None),
            P(("sub", "grp"), None, None, None),
            P(("sub", "grp"), None),
            P(("sub", "grp"), None, None),
            P(("sub", "grp"), None, None, None),
            P(("sub", "grp"), None),
            P("grp", None, None, None),
            P("grp", None),
        ),
        out_specs=P(("sub", "grp"), None),
        check_vma=False,
    )
```

time: 428 us -> 92.2 us (0.22)
  blocking collectives: 265 us -> 0 us
  Pallas kernels: 0 us -> 79.9 us
  matrix products: 44.5 us -> 0 us
  local copies, waits for them, and re-layouts: 51.3 us -> 10.4 us
  starting transfers between devices: 24.9 us -> 0 us
  waiting for transfers between devices: 24.9 us -> 0 us
  other arithmetic: 15.1 us -> 1.37 us
    all_gather x12 -> x0, blocking collectives: 265 us -> none  [the longest x4 122 us: per_device(): group_lifted = lax.all_gather(lifted[None], 'sub', axis=0, tiled=True)]
    pallas_call x0 -> x1, Pallas kernels: none -> 79.9 us  [per_device(): pl.pallas_call(functools.partial(kernel, groups, group_devs), out_shape=j...]
    dot_general x32 -> x0, matrix products: 44.5 us -> none  [the longest x4 25.7 us: per_device(): jnp.einsum('lkij,lkjp->lip', near_tiles, jnp.take(window_vec, near_local,...]
    gather x20 -> x0, local copies, waits for them, and re-layouts: 36.5 us -> none  [the longest x8 29.4 us: per_device(): jnp.take(window_vec, near_local, axis=0)]
    ppermute x16 -> x0, starting transfers between devices: 24.9 us -> none  [from_behind(): return lax.ppermute(value, axis, pairs)]
    ppermute x16 -> x0, waiting for transfers between devices: 24.9 us -> none  [from_behind(): return lax.ppermute(value, axis, pairs)]
    add x4 -> x0, local copies, waits for them, and re-layouts: 8.2 us -> none  [per_device(): near_part + far_part]
    unnamed x48 -> x18, local copies, waits for them, and re-layouts: 1.16 us -> 8.85 us
  transfers between devices with their start and end apart: 16 -> 0, of which waited for: 9 -> 0; matrix products, arithmetic and copies ran while one was open for 3% -> 0% of each run, Pallas kernels for 0% -> 0%
where the time goes in v1:
time: 92.2 us; the launch traced here: 91.7 us
  Pallas kernels  79.9 us (87%)
  local copies, waits for them, and re-layouts  10.4 us (11%)
  other arithmetic  1.37 us (1%)
    pallas_call x1, Pallas kernels, per_device(): pl.pallas_call(functools.partial(kernel, groups, group_devs), out_shape=j...  79.9 us
    unnamed x18, local copies, waits for them, and re-layouts  8.85 us

profile of v1, /device:TPU:0, one launch (start us, length us, event | category | flops | bytes accessed | tf_op | source)
XLA Modules:
  0.0 91.7 jit_solution(15798818495133519359)
XLA Ops:
  0.0 0.7 and_select_fusion.fdev_ref
  0.7 0.7 add_select_fusion.1.near_ref
  1.4 0.8 copy.15
  2.1 1.6 %reshape.12.noise_ref = f32[8,256,1]{2,1,0:T(8,128)S(1)} reshape(f32[2048]{0:T(1024)} %param.14) | data formatting | bytes 16384 | tf_op jit(solution)/shard_map/reshape | solution.py:341
  3.7 0.0 copy-start
  3.7 1.2 %copy-done = f32[2048,128]{1,0:T(8,128)S(1)} copy-done((f32[2048,128]{1,0:T(8,128)S(1)}, f32[2048,128]{1,0:T(8,128)}, u32[]{:S(2)}) %copy-start) | copy-done | bytes 1048600
  4.9 0.0 copy-start.1
  4.9 1.0 %copy-done.1 = bf16[8,4,64,64]{3,2,1,0:T(8,128)(2,1)S(1)} copy-done((bf16[8,4,64,64]{3,2,1,0:T(8,128)(2,1)S(1)}, bf16[8,4,64,64]{3,2,1,0:T(8,128)(2,1)}, u32[]{:S(2)}) %copy-start.1) | copy-done | bytes 262168
  6.0 0.0 copy-start.2
  6.0 0.9 %copy-done.2 = bf16[8,64,256]{2,1,0:T(8,128)(2,1)S(1)} copy-done((bf16[8,64,256]{2,1,0:T(8,128)(2,1)S(1)}, bf16[8,64,256]{2,1,0:T(8,128)(2,1)}, u32[]{:S(2)}) %copy-start.2) | copy-done | bytes 262168
  6.9 0.0 copy-start.3
  6.9 0.9 copy-done.3
  7.8 0.0 copy-start.4
  7.8 0.8 copy-done.4
  8.7 0.0 copy-start.5
  8.7 0.8 copy-done.5
  9.5 0.0 copy-start.6
  9.5 0.7 copy-done.6
  10.2 0.0 copy-start.7
  10.2 0.7 copy-done.7
  10.8 79.9 %shard_map.127 = f32[8,256,128]{2,1,0:T(8,128)S(1)} custom-call(s32[8,6]{1,0:T(8,128)S(1)} %add_select_fusion.1.near_ref, s32[8,4]{1,0:T(8,128)S(1)} %add_select_fusion.far_ref, s32[1,4]{1,0:T(1,128)S(1)} %and_select_fusion.fdev_ref, s32[1,3]{1,0:T(1,128)S(1)} %copy-done.7, f32[8,256,128]{2,1,0:T(8,128)S(1)} %bitcast.3, f32[8,256,1]{2,1,0:T(8,128)S(1)} %reshape.12.noise_ref, ...), custom_call_target="tpu_custom_call" | custom-call | tf_op jit(solution)/shard_map/pallas_call | solution.py:326
  90.7 1.0 %copy.18 = f32[2048,128]{1,0:T(8,128)} copy(f32[2048,128]{1,0:T(8,128)S(1)} %bitcast.2) | data formatting | bytes 2097152
  (1 shorter events, 0.0 us)
Async XLA Ops:
  3.7 1.2 %copy-start = (f32[2048,128]{1,0:T(8,128)S(1)}, f32[2048,128]{1,0:T(8,128)}, u32[]{:S(2)}) copy-start(f32[2048,128]{1,0:T(8,128)} %param.13) | copy-start | bytes 3145732
  4.9 1.0 %copy-start.1 = (bf16[8,4,64,64]{3,2,1,0:T(8,128)(2,1)S(1)}, bf16[8,4,64,64]{3,2,1,0:T(8,128)(2,1)}, u32[]{:S(2)}) copy-start(bf16[8,4,64,64]{3,2,1,0:T(8,128)(2,1)} %lc_ref.1) | copy-start | bytes 786436
  6.0 0.9 %copy-start.2 = (bf16[8,64,256]{2,1,0:T(8,128)(2,1)S(1)}, bf16[8,64,256]{2,1,0:T(8,128)(2,1)}, u32[]{:S(2)}) copy-start(bf16[8,64,256]{2,1,0:T(8,128)(2,1)} %basis_ref.1) | copy-start | bytes 786436
  6.9 0.9 copy-start.3
  7.8 0.8 copy-start.4
  8.7 0.8 copy-start.5
  9.5 0.7 copy-start.6
  10.2 0.7 copy-start.7

commit v2 on v1

v2 whole, which is shorter than its diff:
```python
import functools

import jax
import jax.numpy as jnp
from jax import lax
from jax.experimental import pallas as pl
from jax.experimental.pallas import tpu as pltpu
from jax.sharding import PartitionSpec as P

SPAN = 6
ITERS = 4
MID_DEVS = 8
MESH = pl.DeviceIdType.MESH


relax_step = 0.3


def dot(a, b):
    return jnp.dot(a, b, preferred_element_type=jnp.float32)


def flip(a):
    return a.astype(jnp.float32).T.astype(jnp.bfloat16)


def kernel(
    groups,
    group_devs,
    near_hbm,
    far_hbm,
    fdev_hbm,
    fmid_hbm,
    rhs_hbm,
    noise_hbm,
    basis_hbm,
    lt_hbm,
    lc_hbm,
    dt_hbm,
    dc_hbm,
    mc_hbm,
    tiles_hbm,
    x_ref,
    near_raw,
    far_raw,
    fdev_ref,
    fmid_ref,
    near_ref,
    far_ref,
    rhs_ref,
    noise_raw,
    basis_ref,
    lt_ref,
    lc_ref,
    dt_ref,
    dc_ref,
    mc_ref,
    tiles,
    noise_ref,
    basis_t,
    lt_t,
    dt_t,
    cwin,
    nbasis,
    dt_all,
    gath_here,
    mid_here,
    image_ref,
    win,
    out,
    inc,
    gath,
    mid,
    in_sem,
    tile_sem,
    halo_send,
    halo_recv,
    nb_send,
    nb_recv,
    dt_send,
    dt_recv,
    g_send,
    g_recv,
    m_send,
    m_recv,
):
    leaves, size, probes = rhs_ref.shape
    near = near_ref.shape[1]
    nfar = far_ref.shape[0]
    nfdev = fdev_ref.shape[1]
    nfmid = fmid_ref.shape[1]
    mid_grp = group_devs // MID_DEVS
    count = groups * group_devs
    sub = lax.axis_index("sub")
    grp = lax.axis_index("grp")
    me = sub * groups + grp
    nxt = lax.rem(me + 1, count)
    prv = lax.rem(me + count - 1, count)
    next_id = (nxt // groups, lax.rem(nxt, groups))
    prev_id = (prv // groups, lax.rem(prv, groups))

    operands = [
        (rhs_hbm, rhs_ref),
        (basis_hbm, basis_ref),
        (dt_hbm, dt_ref),
        (lt_hbm, lt_ref),
        (near_hbm, near_raw),
        (far_hbm, far_raw),
        (fdev_hbm, fdev_ref),
        (fmid_hbm, fmid_ref),
        (noise_hbm, noise_raw),
        (lc_hbm, lc_ref),
        (dc_hbm, dc_ref),
        (mc_hbm, mc_ref),
    ]
    loads = [
        pltpu.make_async_copy(src, dst, in_sem.at[i]) for i, (src, dst) in enumerate(operands)
    ]
    for load in loads:
        load.start()
    tile_loads = [
        pltpu.make_async_copy(tiles_hbm.at[l], tiles.at[l], tile_sem.at[l]) for l in range(leaves)
    ]
    for load in tile_loads:
        load.start()

    def sub_peer(j):
        return lax.rem(sub + j, group_devs)

    def grp_peer(j):
        return lax.rem(grp + j, groups)

    def remote(src, dst, send, recv, device):
        return pltpu.make_async_remote_copy(
            src_ref=src,
            dst_ref=dst,
            send_sem=send,
            recv_sem=recv,
            device_id=device,
            device_id_type=MESH,
        )

    def to_prev(it, h):
        return remote(
            out.at[it, h],
            inc.at[it, SPAN + h],
            halo_send.at[it, 0, h],
            halo_recv.at[it, 0, h],
            prev_id,
        )

    def to_next(it, h):
        return remote(
            out.at[it, leaves - SPAN + h],
            inc.at[it, h],
            halo_send.at[it, 1, h],
            halo_recv.at[it, 1, h],
            next_id,
        )

    def basis_copy(side):
        if side == 0:
            src, dst, device = basis_ref.at[pl.ds(0, SPAN)], nbasis.at[pl.ds(SPAN, SPAN)], prev_id
        else:
            src, dst, device = (
                basis_ref.at[pl.ds(leaves - SPAN, SPAN)],
                nbasis.at[pl.ds(0, SPAN)],
                next_id,
            )
        return remote(src, dst, nb_send.at[side], nb_recv.at[side], device)

    def dt_copy(j, owner):
        return remote(
            dt_ref.at[0], dt_all.at[owner], dt_send.at[j], dt_recv.at[j], (sub_peer(j), grp)
        )

    def gath_copy(it, j, owner):
        block = gath.at[it, owner]
        return remote(block, block, g_send.at[it, j], g_recv.at[it, j], (sub_peer(j), grp))

    def mid_copy(it, j, owner):
        block = mid.at[it, pl.ds(owner * mid_grp, mid_grp)]
        return remote(block, block, m_send.at[it, j], m_recv.at[it, j], (sub, grp_peer(j)))

    early = SPAN // 2
    middle = early + 1
    prev_order = list(range(SPAN))
    next_order = list(range(SPAN - 1, -1, -1))
    prev_early, next_early = prev_order[:early], next_order[:early]
    ready = [
        l
        for l in range(leaves)
        if l >= SPAN - middle and l + SPAN - leaves < middle
    ]
    first = [h for h in range(SPAN) if h in prev_early]
    last = [leaves - SPAN + h for h in next_early]
    order = []
    for pair in zip(reversed(first), reversed(last)):
        order += [l for l in pair if l not in order]
    order += [l for l in range(leaves) if l not in order]

    def stage(it, step):
        h = next_order[step]
        to_next(it, h).wait_recv()
        block = inc[it, h]
        win[h] = block
        cwin[h] = dot(nbasis[h], block).astype(jnp.bfloat16)
        h = prev_order[step]
        to_prev(it, h).wait_recv()
        block = inc[it, SPAN + h]
        win[SPAN + leaves + h] = block
        cwin[SPAN + leaves + h] = dot(nbasis[SPAN + h], block).astype(jnp.bfloat16)

    def near_part(l):
        image = dot(tiles[l, 0], win[near_ref[l, 0]])
        for k in range(1, near):
            image = image + dot(tiles[l, k], win[near_ref[l, k]])
        return image

    barrier = pltpu.get_barrier_semaphore()
    for device in (prev_id, next_id):
        pl.semaphore_signal(barrier, inc=1, device_id=device, device_id_type=MESH)
    for j in range(1, group_devs):
        pl.semaphore_signal(barrier, inc=1, device_id=(sub_peer(j), grp), device_id_type=MESH)
    for j in range(1, groups):
        pl.semaphore_signal(barrier, inc=1, device_id=(sub, grp_peer(j)), device_id_type=MESH)

    loads[0].wait()
    for l in range(leaves):
        start = relax_step * rhs_ref[l]
        x_ref[l] = start
        out[0, l] = start.astype(jnp.bfloat16)
    pl.semaphore_wait(barrier, 2 + (group_devs - 1) + (groups - 1))

    for h in prev_early:
        to_prev(0, h).start()
    for h in next_early:
        to_next(0, h).start()
    for load in loads[1:]:
        load.wait()
    for j in range(1, group_devs):
        dt_copy(j, sub).start()
    basis_copy(0).start()
    basis_copy(1).start()

    total_leaves = leaves * count
    window = leaves + 2 * SPAN
    for l in range(leaves):
        for k in range(near):
            place = near_raw[l, k] - me * leaves + SPAN
            place = jnp.where(place < 0, place + total_leaves, place)
            place = jnp.where(place >= total_leaves, place - total_leaves, place)
            near_ref[l, k] = jnp.minimum(place, window - 1)
        for k in range(nfar):
            place = far_raw[k, l] - me * leaves + SPAN
            place = jnp.where(place < 0, place + total_leaves, place)
            place = jnp.where(place >= total_leaves, place - total_leaves, place)
            far_ref[k, l] = jnp.minimum(place, window - 1)

    dt_all[sub] = dt_ref[0]
    dt_t[...] = flip(dt_ref[0])
    lanes = noise_raw.shape[1]
    pieces = size // lanes
    for l in range(leaves):
        basis_t[l] = flip(basis_ref[l])
        lt_t[l] = flip(lt_ref[l])
        for c in range(pieces):
            row = noise_raw[pl.ds(l * pieces + c, 1), :]
            noise_ref[l, pl.ds(c * lanes, lanes), :] = jnp.broadcast_to(row, (probes, lanes)).T
    for j in range(1, group_devs):
        dt_copy(j, lax.rem(sub + group_devs - j, group_devs)).wait_recv()
    for load in tile_loads:
        load.wait()

    def sweep(it, carry):
        total = None
        for l in range(leaves):
            block = out[it, l]
            win[SPAN + l] = block
            coef = dot(basis_ref[l], block).astype(jnp.bfloat16)
            cwin[SPAN + l] = coef
            term = dot(lt_ref[l], coef)
            total = term if total is None else total + term
        gath[it, sub] = total.astype(jnp.bfloat16)
        for j in range(1, group_devs):
            gath_copy(it, j, sub).start()
        for step in range(early, middle):
            to_prev(it, prev_order[step]).start()
            to_next(it, next_order[step]).start()

        for j in range(1, group_devs):
            gath_copy(it, j, lax.rem(sub + group_devs - j, group_devs)).wait_recv()
        for m in range(mid_grp):
            lifted = None
            for s in range(MID_DEVS):
                place = m * MID_DEVS + s
                coef = gath[it, place]
                gath_here[place] = coef
                term = dot(dt_all[place], coef).astype(jnp.bfloat16).astype(jnp.float32)
                lifted = term if lifted is None else lifted + term
            mid[it, grp * mid_grp + m] = lifted.astype(jnp.bfloat16)
        for j in range(1, groups):
            mid_copy(it, j, grp).start()
        for step in range(middle, SPAN):
            to_prev(it, prev_order[step]).start()
            to_next(it, next_order[step]).start()

        dev_total = None
        for k in range(nfdev):
            term = dot(dc_ref[0, k], gath_here[lax.div(fdev_ref[0, k], groups)])
            dev_total = term if dev_total is None else dev_total + term

        @pl.when(it == 0)
        def _():
            basis_copy(0).wait_recv()
            basis_copy(1).wait_recv()

        for step in range(middle):
            stage(it, step)
        for l in ready:
            image_ref[l] = near_part(l)

        for j in range(1, groups):
            mid_copy(it, j, lax.rem(grp + groups - j, groups)).wait_recv()
        for m in range(groups * mid_grp):
            mid_here[m] = mid[it, m]
        own_mid = sub // MID_DEVS
        field = None
        for k in range(nfmid):
            term = dot(mc_ref[own_mid, k], mid_here[fmid_ref[own_mid, k]])
            field = term if field is None else field + term
        dev_field = (dev_total + dot(dt_t[...], field.astype(jnp.bfloat16))).astype(jnp.bfloat16)

        for step in range(middle, SPAN):
            stage(it, step)

        for l in order:
            acc = dot(lt_t[l], dev_field)
            for k in range(nfar):
                acc = acc + dot(lc_ref[l, k], cwin[far_ref[k, l]])
            image = image_ref[l] if l in ready else near_part(l)
            image = image + dot(basis_t[l], acc.astype(jnp.bfloat16))
            old = x_ref[l]
            image = image + noise_ref[l] * old
            new = old + relax_step * (rhs_ref[l] - image)
            x_ref[l] = new

            @pl.when(it + 1 < ITERS)
            def _():
                out[it + 1, l] = new.astype(jnp.bfloat16)
                if l in first:
                    to_prev(it + 1, l).start()
                if l in last:
                    to_next(it + 1, l - (leaves - SPAN)).start()

        return carry

    lax.fori_loop(0, ITERS, sweep, 0)

    for j in range(1, group_devs):
        dt_copy(j, sub).wait_send()
    basis_copy(0).wait_send()
    basis_copy(1).wait_send()

    def drain(it, carry):
        for h in range(SPAN):
            to_prev(it, h).wait_send()
            to_next(it, h).wait_send()
        for j in range(1, group_devs):
            gath_copy(it, j, sub).wait_send()
        for j in range(1, groups):
            mid_copy(it, j, grp).wait_send()
        return carry

    lax.fori_loop(0, ITERS, drain, 0)


def per_device(
    right_side,
    noise_var,
    near_tiles,
    near_index,
    leaf_basis,
    leaf_transfer,
    leaf_coupling,
    far_leaf,
    dev_transfer,
    dev_coupling,
    far_dev,
    mid_coupling,
    far_mid,
):
    leaves, near, size, _ = near_tiles.shape
    probes = right_side.shape[1]
    rank = leaf_basis.shape[1]
    groups = lax.axis_size("grp")
    group_devs = lax.axis_size("sub")
    window = leaves + 2 * SPAN
    all_mids = groups * (group_devs // MID_DEVS)
    bf16, f32, i32 = jnp.bfloat16, jnp.float32, jnp.int32
    dma = pltpu.SemaphoreType.DMA
    operands = [
        near_index,
        far_leaf.T,
        far_dev,
        far_mid,
        right_side.reshape(leaves, size, probes),
        noise_var.reshape(-1, probes),
        leaf_basis,
        leaf_transfer,
        leaf_coupling,
        dev_transfer,
        dev_coupling,
        mid_coupling,
        near_tiles,
    ]
    scratch = [pltpu.SMEM(a.shape, i32) for a in operands[:4]]
    scratch += [pltpu.SMEM(a.shape, i32) for a in operands[:2]]
    scratch += [pltpu.VMEM(a.shape, a.dtype) for a in operands[4:]]
    scratch += [
        pltpu.VMEM((leaves, size, probes), f32),
        pltpu.VMEM((leaves, size, rank), bf16),
        pltpu.VMEM((leaves, rank, rank), bf16),
        pltpu.VMEM((rank, rank), bf16),
        pltpu.VMEM((window, rank, probes), bf16),
        pltpu.VMEM((2 * SPAN, rank, size), bf16),
        pltpu.VMEM((group_devs, rank, rank), bf16),
        pltpu.VMEM((group_devs, rank, probes), bf16),
        pltpu.VMEM((all_mids, rank, probes), bf16),
        pltpu.VMEM((leaves, size, probes), f32),
        pltpu.VMEM((window, size, probes), bf16),
        pltpu.VMEM((ITERS, leaves, size, probes), bf16),
        pltpu.VMEM((ITERS, 2 * SPAN, size, probes), bf16),
        pltpu.VMEM((ITERS, group_devs, rank, probes), bf16),
        pltpu.VMEM((ITERS, all_mids, rank, probes), bf16),
        dma((12,)),
        dma((leaves,)),
        dma((ITERS, 2, SPAN)),
        dma((ITERS, 2, SPAN)),
        dma((2,)),
        dma((2,)),
        dma((group_devs,)),
        dma((group_devs,)),
        dma((ITERS, group_devs)),
        dma((ITERS, group_devs)),
        dma((ITERS, groups)),
        dma((ITERS, groups)),
    ]
    result = pl.pallas_call(
        functools.partial(kernel, groups, group_devs),
        out_shape=jax.ShapeDtypeStruct((leaves, size, probes), f32),
        in_specs=[pl.BlockSpec(memory_space=pl.ANY)] * len(operands),
        out_specs=pl.BlockSpec(memory_space=pltpu.VMEM),
        scratch_shapes=scratch,
        compiler_params=pltpu.CompilerParams(
            collective_id=0, has_side_effects=True, vmem_limit_bytes=56 * 1024 * 1024
        ),
    )(*operands)
    return result.reshape(leaves * size, probes)


def solution(mesh):
    return jax.shard_map(
        per_device,
        mesh=mesh,
        in_specs=(
            P(("sub", "grp"), None),
            P(("sub", "grp")),
            P(("sub", "grp"), None, None, None),
            P(("sub", "grp"), None),
            P(("sub", "grp"), None, None),
            P(("sub", "grp"), None, None),
            P(("sub", "grp"), None, None, None),
            P(("sub", "grp"), None),
            P(("sub", "grp"), None, None),
            P(("sub", "grp"), None, None, None),
            P(("sub", "grp"), None),
            P("grp", None, None, None),
            P("grp", None),
        ),
        out_specs=P(("sub", "grp"), None),
        check_vma=False,
    )
```

time: 92.2 us -> 74.5 us (0.81)
  local copies, waits for them, and re-layouts: 10.4 us -> 2.26 us
  Pallas kernels: 79.9 us -> 71.9 us
  other arithmetic: 1.37 us -> 0 us
    pallas_call x1, Pallas kernels: 79.9 us -> 71.9 us  [per_device(): pl.pallas_call(functools.partial(kernel, groups, group_devs), out_shape=j...]
    unnamed x18 -> x1, local copies, waits for them, and re-layouts: 8.85 us -> 2.26 us
    reshape x1 -> x0, local copies, waits for them, and re-layouts: 1.56 us -> none  [per_device(): noise_var.reshape(leaves, size, 1)]
    select_n x3 -> x0, other arithmetic: 1.37 us -> none  [the longest x1 0.7 us: per_device(): near_local = jnp.mod(near_index - first_leaf + SPAN, total_leaves)]
where the time goes in v2:
time: 74.5 us; the launch traced here: 74.2 us
  Pallas kernels  71.9 us (97%)
  local copies, waits for them, and re-layouts  2.26 us (3%)
    pallas_call x1, Pallas kernels, per_device(): pl.pallas_call(functools.partial(kernel, groups, group_devs), out_shape=j...  71.9 us
    unnamed x1, local copies, waits for them, and re-layouts  2.26 us

profile of v2, /device:TPU:0, one launch (start us, length us, event | category | flops | bytes accessed | tf_op | source)
XLA Modules:
  0.0 74.2 jit_solution(15581681221462853266)
XLA Ops:
  0.0 71.9 %shard_map.127 = f32[8,256,128]{2,1,0:T(8,128)} custom-call(s32[8,6]{1,0:T(8,128)} %near_hbm.1, s32[4,8]{1,0:T(4,128)} %bitcast.7, s32[1,4]{1,0:T(1,128)} %fdev_hbm.1, s32[1,3]{1,0:T(1,128)} %fmid_hbm.1, f32[8,256,128]{2,1,0:T(8,128)} %bitcast.5, f32[16,128]{1,0:T(8,128)} %bitcast.6, bf16[8,64,256]{2,1,0:T(8,128)(2,1)} %basis_hbm.1, ...), custom_call_target="tpu_custom_call" | custom-call | tf_op jit(solution)/shard_map/pallas_call | solution.py:449
  71.9 2.3 %copy.15 = f32[2048,128]{1,0:T(8,128)} copy(f32[2048,128]{1,0:T(8,128)} %bitcast.4) | data formatting | bytes 2097152

commit v3 on v2

--- a/solution.py
+++ b/solution.py
@@ -58,7 +58,8 @@
     tiles,
     noise_ref,
     basis_t,
-    lt_t,
+    far_all,
+    field_ref,
     dt_t,
     cwin,
     nbasis,
@@ -85,6 +86,7 @@
     m_recv,
 ):
     leaves, size, probes = rhs_ref.shape
+    rank = basis_ref.shape[1]
     near = near_ref.shape[1]
     nfar = far_ref.shape[0]
     nfdev = fdev_ref.shape[1]
@@ -183,21 +185,19 @@
         return remote(block, block, m_send.at[it, j], m_recv.at[it, j], (sub, grp_peer(j)))
 
     early = SPAN // 2
-    middle = early + 1
+    middle = SPAN - 1
     prev_order = list(range(SPAN))
     next_order = list(range(SPAN - 1, -1, -1))
-    prev_early, next_early = prev_order[:early], next_order[:early]
-    ready = [
-        l
-        for l in range(leaves)
-        if l >= SPAN - middle and l + SPAN - leaves < middle
-    ]
-    first = [h for h in range(SPAN) if h in prev_early]
-    last = [leaves - SPAN + h for h in next_early]
-    order = []
-    for pair in zip(reversed(first), reversed(last)):
-        order += [l for l in pair if l not in order]
-    order += [l for l in range(leaves) if l not in order]
+    first = prev_order[:early]
+    last = [leaves - SPAN + h for h in next_order[:early]]
+
+    def steps_needed(l):
+        return min(SPAN, max(0, SPAN - l, l + SPAN - leaves + 1))
+
+    by_step = [[l for l in range(leaves) if steps_needed(l) == n] for n in range(SPAN + 1)]
+
+    def sends_first(batch):
+        return sorted(batch, key=lambda l: (l not in first and l not in last, l))
 
     def stage(it, step):
         h = next_order[step]
@@ -232,10 +232,9 @@
         out[0, l] = start.astype(jnp.bfloat16)
     pl.semaphore_wait(barrier, 2 + (group_devs - 1) + (groups - 1))
 
-    for h in prev_early:
-        to_prev(0, h).start()
-    for h in next_early:
-        to_next(0, h).start()
+    for step in range(early):
+        to_prev(0, prev_order[step]).start()
+        to_next(0, next_order[step]).start()
     for load in loads[1:]:
         load.wait()
     for j in range(1, group_devs):
@@ -263,7 +262,9 @@
     pieces = size // lanes
     for l in range(leaves):
         basis_t[l] = flip(basis_ref[l])
-        lt_t[l] = flip(lt_ref[l])
+        for k in range(nfar):
+            far_all[l, :, pl.ds(k * rank, rank)] = lc_ref[l, k]
+        far_all[l, :, pl.ds(nfar * rank, rank)] = flip(lt_ref[l])
         for c in range(pieces):
             row = noise_raw[pl.ds(l * pieces + c, 1), :]
             noise_ref[l, pl.ds(c * lanes, lanes), :] = jnp.broadcast_to(row, (probes, lanes)).T
@@ -287,6 +288,23 @@
         for step in range(early, middle):
             to_prev(it, prev_order[step]).start()
             to_next(it, next_order[step]).start()
+
+        @pl.when(it == 0)
+        def _():
+            basis_copy(0).wait_recv()
+            basis_copy(1).wait_recv()
+
+        def arrive(steps):
+            for step in steps:
+                if step < SPAN:
+                    stage(it, step)
+            for step in steps:
+                for l in by_step[step + 1]:
+                    image_ref[l] = near_part(l)
+
+        for l in by_step[0]:
+            image_ref[l] = near_part(l)
+        arrive(range(early))
 
         for j in range(1, group_devs):
             gath_copy(it, j, lax.rem(sub + group_devs - j, group_devs)).wait_recv()
@@ -310,15 +328,7 @@
             term = dot(dc_ref[0, k], gath_here[lax.div(fdev_ref[0, k], groups)])
             dev_total = term if dev_total is None else dev_total + term
 
-        @pl.when(it == 0)
-        def _():
-            basis_copy(0).wait_recv()
-            basis_copy(1).wait_recv()
-
-        for step in range(middle):
-            stage(it, step)
-        for l in ready:
-            image_ref[l] = near_part(l)
+        arrive(range(early, middle))
 
         for j in range(1, groups):
             mid_copy(it, j, lax.rem(grp + groups - j, groups)).wait_recv()
@@ -331,28 +341,33 @@
             field = term if field is None else field + term
         dev_field = (dev_total + dot(dt_t[...], field.astype(jnp.bfloat16))).astype(jnp.bfloat16)
 
-        for step in range(middle, SPAN):
-            stage(it, step)
-
-        for l in order:
-            acc = dot(lt_t[l], dev_field)
-            for k in range(nfar):
-                acc = acc + dot(lc_ref[l, k], cwin[far_ref[k, l]])
-            image = image_ref[l] if l in ready else near_part(l)
-            image = image + dot(basis_t[l], acc.astype(jnp.bfloat16))
-            old = x_ref[l]
-            image = image + noise_ref[l] * old
-            new = old + relax_step * (rhs_ref[l] - image)
-            x_ref[l] = new
-
-            @pl.when(it + 1 < ITERS)
-            def _():
-                out[it + 1, l] = new.astype(jnp.bfloat16)
-                if l in first:
-                    to_prev(it + 1, l).start()
-                if l in last:
-                    to_next(it + 1, l - (leaves - SPAN)).start()
-
+        def finish(batch):
+            for l in batch:
+                parts = [cwin[far_ref[k, l]] for k in range(nfar)] + [dev_field]
+                field_ref[l] = dot(far_all[l], jnp.concatenate(parts, axis=0)).astype(jnp.bfloat16)
+            for at in range(0, len(batch), 2):
+                pair = batch[at : at + 2]
+                for l in pair:
+                    image = image_ref[l] + dot(basis_t[l], field_ref[l])
+                    old = x_ref[l]
+                    image = image + noise_ref[l] * old
+                    new = old + relax_step * (rhs_ref[l] - image)
+                    x_ref[l] = new
+                    out[it + 1, l] = new.astype(jnp.bfloat16)
+                if any(l in first or l in last for l in pair):
+
+                    @pl.when(it + 1 < ITERS)
+                    def _():
+                        for l in pair:
+                            if l in first:
+                                to_prev(it + 1, l).start()
+                            if l in last:
+                                to_next(it + 1, l - (leaves - SPAN)).start()
+
+        done = [l for step in range(middle + 1) for l in reversed(by_step[step])]
+        finish(sends_first(done))
+        arrive(range(middle, SPAN))
+        finish(sends_first([l for l in range(leaves) if l not in done]))
         return carry
 
     lax.fori_loop(0, ITERS, sweep, 0)
@@ -420,7 +435,8 @@
     scratch += [
         pltpu.VMEM((leaves, size, probes), f32),
         pltpu.VMEM((leaves, size, rank), bf16),
-        pltpu.VMEM((leaves, rank, rank), bf16),
+        pltpu.VMEM((leaves, rank, (far_leaf.shape[1] + 1) * rank), bf16),
+        pltpu.VMEM((leaves, rank, probes), bf16),
         pltpu.VMEM((rank, rank), bf16),
         pltpu.VMEM((window, rank, probes), bf16),
         pltpu.VMEM((2 * SPAN, rank, size), bf16),
@@ -429,7 +445,7 @@
         pltpu.VMEM((all_mids, rank, probes), bf16),
         pltpu.VMEM((leaves, size, probes), f32),
         pltpu.VMEM((window, size, probes), bf16),
-        pltpu.VMEM((ITERS, leaves, size, probes), bf16),
+        pltpu.VMEM((ITERS + 1, leaves, size, probes), bf16),
         pltpu.VMEM((ITERS, 2 * SPAN, size, probes), bf16),
         pltpu.VMEM((ITERS, group_devs, rank, probes), bf16),
         pltpu.VMEM((ITERS, all_mids, rank, probes), bf16),

time: 74.5 us -> 70.1 us (0.941)
  Pallas kernels: 71.9 us -> 67.7 us
    pallas_call x1, Pallas kernels: 71.9 us -> 67.7 us  [per_device(): pl.pallas_call(functools.partial(kernel, groups, group_devs), out_shape=j...]
where the time goes in v3:
time: 70.1 us; the launch traced here: 70 us
  Pallas kernels  67.7 us (97%)
  local copies, waits for them, and re-layouts  2.26 us (3%)
    pallas_call x1, Pallas kernels, per_device(): pl.pallas_call(functools.partial(kernel, groups, group_devs), out_shape=j...  67.7 us
    unnamed x1, local copies, waits for them, and re-layouts  2.26 us

profile of v3, /device:TPU:0, one launch (start us, length us, event | category | flops | bytes accessed | tf_op | source)
XLA Modules:
  0.0 70.0 jit_solution(15372369740519546408)
XLA Ops:
  0.0 67.7 %shard_map.127 = f32[8,256,128]{2,1,0:T(8,128)} custom-call(s32[8,6]{1,0:T(8,128)} %near_hbm.1, s32[4,8]{1,0:T(4,128)} %bitcast.7, s32[1,4]{1,0:T(1,128)} %fdev_hbm.1, s32[1,3]{1,0:T(1,128)} %fmid_hbm.1, f32[8,256,128]{2,1,0:T(8,128)} %bitcast.5, f32[16,128]{1,0:T(8,128)} %bitcast.6, bf16[8,64,256]{2,1,0:T(8,128)(2,1)} %basis_hbm.1, ...), custom_call_target="tpu_custom_call" | custom-call | tf_op jit(solution)/shard_map/pallas_call | solution.py:465
  67.7 2.3 %copy.15 = f32[2048,128]{1,0:T(8,128)} copy(f32[2048,128]{1,0:T(8,128)} %bitcast.4) | data formatting | bytes 2097152

commit v4 on v3

--- a/solution.py
+++ b/solution.py
@@ -185,7 +185,7 @@
         return remote(block, block, m_send.at[it, j], m_recv.at[it, j], (sub, grp_peer(j)))
 
     early = SPAN // 2
-    middle = SPAN - 1
+    middle = early + 1
     prev_order = list(range(SPAN))
     next_order = list(range(SPAN - 1, -1, -1))
     first = prev_order[:early]
@@ -199,17 +199,16 @@
     def sends_first(batch):
         return sorted(batch, key=lambda l: (l not in first and l not in last, l))
 
-    def stage(it, step):
-        h = next_order[step]
-        to_next(it, h).wait_recv()
-        block = inc[it, h]
-        win[h] = block
-        cwin[h] = dot(nbasis[h], block).astype(jnp.bfloat16)
-        h = prev_order[step]
-        to_prev(it, h).wait_recv()
-        block = inc[it, SPAN + h]
-        win[SPAN + leaves + h] = block
-        cwin[SPAN + leaves + h] = dot(nbasis[SPAN + h], block).astype(jnp.bfloat16)
+    def stage(it, steps):
+        for step in steps:
+            to_next(it, next_order[step]).wait_recv()
+            to_prev(it, prev_order[step]).wait_recv()
+        for step in steps:
+            for h in (next_order[step], SPAN + prev_order[step]):
+                place = h if h < SPAN else leaves + h
+                block = inc[it, h]
+                win[place] = block
+                cwin[place] = dot(nbasis[h], block).astype(jnp.bfloat16)
 
     def near_part(l):
         image = dot(tiles[l, 0], win[near_ref[l, 0]])
@@ -295,9 +294,7 @@
             basis_copy(1).wait_recv()
 
         def arrive(steps):
-            for step in steps:
-                if step < SPAN:
-                    stage(it, step)
+            stage(it, steps)
             for step in steps:
                 for l in by_step[step + 1]:
                     image_ref[l] = near_part(l)
@@ -366,28 +363,26 @@
 
         done = [l for step in range(middle + 1) for l in reversed(by_step[step])]
         finish(sends_first(done))
-        arrive(range(middle, SPAN))
-        finish(sends_first([l for l in range(leaves) if l not in done]))
-        return carry
-
-    lax.fori_loop(0, ITERS, sweep, 0)
-
-    for j in range(1, group_devs):
-        dt_copy(j, sub).wait_send()
-    basis_copy(0).wait_send()
-    basis_copy(1).wait_send()
-
-    def drain(it, carry):
-        for h in range(SPAN):
-            to_prev(it, h).wait_send()
-            to_next(it, h).wait_send()
+
+        @pl.when(it == 0)
+        def _():
+            for j in range(1, group_devs):
+                dt_copy(j, sub).wait_send()
+            basis_copy(0).wait_send()
+            basis_copy(1).wait_send()
+
         for j in range(1, group_devs):
             gath_copy(it, j, sub).wait_send()
         for j in range(1, groups):
             mid_copy(it, j, grp).wait_send()
+        for h in range(SPAN):
+            to_prev(it, h).wait_send()
+            to_next(it, h).wait_send()
+        arrive(range(middle, SPAN))
+        finish(sends_first([l for l in range(leaves) if l not in done]))
         return carry
 
-    lax.fori_loop(0, ITERS, drain, 0)
+    lax.fori_loop(0, ITERS, sweep, 0)
 
 
 def per_device(

time: 70.1 us -> 71.3 us (1.017)
  Pallas kernels: 67.7 us -> 68.8 us
    pallas_call x1, Pallas kernels: 67.7 us -> 68.8 us  [per_device(): pl.pallas_call(functools.partial(kernel, groups, group_devs), out_shape=j...]
where the time goes in v4:
time: 71.3 us; the launch traced here: 71.1 us
  Pallas kernels  68.8 us (96%)
  local copies, waits for them, and re-layouts  2.26 us (3%)
    pallas_call x1, Pallas kernels, per_device(): pl.pallas_call(functools.partial(kernel, groups, group_devs), out_shape=j...  68.8 us
    unnamed x1, local copies, waits for them, and re-layouts  2.26 us

profile of v4, /device:TPU:0, one launch (start us, length us, event | category | flops | bytes accessed | tf_op | source)
XLA Modules:
  0.0 71.1 jit_solution(9221673935895237283)
XLA Ops:
  0.0 68.8 %shard_map.127 = f32[8,256,128]{2,1,0:T(8,128)} custom-call(s32[8,6]{1,0:T(8,128)} %near_hbm.1, s32[4,8]{1,0:T(4,128)} %bitcast.7, s32[1,4]{1,0:T(1,128)} %fdev_hbm.1, s32[1,3]{1,0:T(1,128)} %fmid_hbm.1, f32[8,256,128]{2,1,0:T(8,128)} %bitcast.5, f32[16,128]{1,0:T(8,128)} %bitcast.6, bf16[8,64,256]{2,1,0:T(8,128)(2,1)} %basis_hbm.1, ...), custom_call_target="tpu_custom_call" | custom-call | tf_op jit(solution)/shard_map/pallas_call | solution.py:460
  68.9 2.3 %copy.15 = f32[2048,128]{1,0:T(8,128)} copy(f32[2048,128]{1,0:T(8,128)} %bitcast.4) | data formatting | bytes 2097152

commit v5 on v4

--- a/solution.py
+++ b/solution.py
@@ -121,7 +121,11 @@
     for load in loads:
         load.start()
     tile_loads = [
-        pltpu.make_async_copy(tiles_hbm.at[l], tiles.at[l], tile_sem.at[l]) for l in range(leaves)
+        pltpu.make_async_copy(
+            tiles_hbm.at[l, k], tiles.at[l, :, pl.ds(k * size, size)], tile_sem.at[l, k]
+        )
+        for l in range(leaves)
+        for k in range(near)
     ]
     for load in tile_loads:
         load.start()
@@ -185,7 +189,7 @@
         return remote(block, block, m_send.at[it, j], m_recv.at[it, j], (sub, grp_peer(j)))
 
     early = SPAN // 2
-    middle = early + 1
+    middle = SPAN - 1
     prev_order = list(range(SPAN))
     next_order = list(range(SPAN - 1, -1, -1))
     first = prev_order[:early]
@@ -211,9 +215,7 @@
                 cwin[place] = dot(nbasis[h], block).astype(jnp.bfloat16)
 
     def near_part(l):
-        image = dot(tiles[l, 0], win[near_ref[l, 0]])
-        for k in range(1, near):
-            image = image + dot(tiles[l, k], win[near_ref[l, k]])
+        image = dot(tiles[l], jnp.concatenate([win[near_ref[l, k]] for k in range(near)], axis=0))
         return image
 
     barrier = pltpu.get_barrier_semaphore()
@@ -426,7 +428,8 @@
     ]
     scratch = [pltpu.SMEM(a.shape, i32) for a in operands[:4]]
     scratch += [pltpu.SMEM(a.shape, i32) for a in operands[:2]]
-    scratch += [pltpu.VMEM(a.shape, a.dtype) for a in operands[4:]]
+    scratch += [pltpu.VMEM(a.shape, a.dtype) for a in operands[4:-1]]
+    scratch += [pltpu.VMEM((leaves, size, near * size), bf16)]
     scratch += [
         pltpu.VMEM((leaves, size, probes), f32),
         pltpu.VMEM((leaves, size, rank), bf16),
@@ -445,7 +448,7 @@
         pltpu.VMEM((ITERS, group_devs, rank, probes), bf16),
         pltpu.VMEM((ITERS, all_mids, rank, probes), bf16),
         dma((12,)),
-        dma((leaves,)),
+        dma((leaves, near)),
         dma((ITERS, 2, SPAN)),
         dma((ITERS, 2, SPAN)),
         dma((2,)),

time: 71.3 us -> 69.7 us (0.978)
  Pallas kernels: 68.8 us -> 66.7 us
    pallas_call x1, Pallas kernels: 68.8 us -> 66.7 us  [per_device(): pl.pallas_call(functools.partial(kernel, groups, group_devs), out_shape=j...]
where the time goes in v5:
time: 69.7 us; the launch traced here: 69 us
  Pallas kernels  66.7 us (96%)
  local copies, waits for them, and re-layouts  2.26 us (3%)
    pallas_call x1, Pallas kernels, per_device(): pl.pallas_call(functools.partial(kernel, groups, group_devs), out_shape=j...  66.7 us
    unnamed x1, local copies, waits for them, and re-layouts  2.26 us

profile of v5, /device:TPU:0, one launch (start us, length us, event | category | flops | bytes accessed | tf_op | source)
XLA Modules:
  0.0 69.0 jit_solution(4849428412520564043)
XLA Ops:
  0.0 66.7 %shard_map.127 = f32[8,256,128]{2,1,0:T(8,128)} custom-call(s32[8,6]{1,0:T(8,128)} %near_hbm.1, s32[4,8]{1,0:T(4,128)} %bitcast.7, s32[1,4]{1,0:T(1,128)} %fdev_hbm.1, s32[1,3]{1,0:T(1,128)} %fmid_hbm.1, f32[8,256,128]{2,1,0:T(8,128)} %bitcast.5, f32[16,128]{1,0:T(8,128)} %bitcast.6, bf16[8,64,256]{2,1,0:T(8,128)(2,1)} %basis_hbm.1, ...), custom_call_target="tpu_custom_call" | custom-call | tf_op jit(solution)/shard_map/pallas_call | solution.py:463
  66.7 2.3 %copy.15 = f32[2048,128]{1,0:T(8,128)} copy(f32[2048,128]{1,0:T(8,128)} %bitcast.4) | data formatting | bytes 2097152

commit v6 on v5

--- a/solution.py
+++ b/solution.py
@@ -275,6 +275,9 @@
         load.wait()
 
     def sweep(it, carry):
+        for step in range(early, SPAN):
+            to_prev(it, prev_order[step]).start()
+            to_next(it, next_order[step]).start()
         total = None
         for l in range(leaves):
             block = out[it, l]
@@ -286,9 +289,6 @@
         gath[it, sub] = total.astype(jnp.bfloat16)
         for j in range(1, group_devs):
             gath_copy(it, j, sub).start()
-        for step in range(early, middle):
-            to_prev(it, prev_order[step]).start()
-            to_next(it, next_order[step]).start()
 
         @pl.when(it == 0)
         def _():
@@ -318,9 +318,6 @@
             mid[it, grp * mid_grp + m] = lifted.astype(jnp.bfloat16)
         for j in range(1, groups):
             mid_copy(it, j, grp).start()
-        for step in range(middle, SPAN):
-            to_prev(it, prev_order[step]).start()
-            to_next(it, next_order[step]).start()
 
         dev_total = None
         for k in range(nfdev):

time: 69.7 us -> 72 us (1.033)
  Pallas kernels: 66.7 us -> 69.6 us
    pallas_call x1, Pallas kernels: 66.7 us -> 69.6 us  [per_device(): pl.pallas_call(functools.partial(kernel, groups, group_devs), out_shape=j...]
where the time goes in v6:
time: 72 us; the launch traced here: 71.9 us
  Pallas kernels  69.6 us (97%)
  local copies, waits for them, and re-layouts  2.26 us (3%)
    pallas_call x1, Pallas kernels, per_device(): pl.pallas_call(functools.partial(kernel, groups, group_devs), out_shape=j...  69.6 us
    unnamed x1, local copies, waits for them, and re-layouts  2.26 us

profile of v6, /device:TPU:0, one launch (start us, length us, event | category | flops | bytes accessed | tf_op | source)
XLA Modules:
  0.0 71.9 jit_solution(16905927062567299453)
XLA Ops:
  0.0 69.6 %shard_map.127 = f32[8,256,128]{2,1,0:T(8,128)} custom-call(s32[8,6]{1,0:T(8,128)} %near_hbm.1, s32[4,8]{1,0:T(4,128)} %bitcast.7, s32[1,4]{1,0:T(1,128)} %fdev_hbm.1, s32[1,3]{1,0:T(1,128)} %fmid_hbm.1, f32[8,256,128]{2,1,0:T(8,128)} %bitcast.5, f32[16,128]{1,0:T(8,128)} %bitcast.6, bf16[8,64,256]{2,1,0:T(8,128)(2,1)} %basis_hbm.1, ...), custom_call_target="tpu_custom_call" | custom-call | tf_op jit(solution)/shard_map/pallas_call | solution.py:460
  69.6 2.3 %copy.15 = f32[2048,128]{1,0:T(8,128)} copy(f32[2048,128]{1,0:T(8,128)} %bitcast.4) | data formatting | bytes 2097152

commit v7 on v5

--- a/solution.py
+++ b/solution.py
@@ -127,8 +127,6 @@
         for l in range(leaves)
         for k in range(near)
     ]
-    for load in tile_loads:
-        load.start()
 
     def sub_peer(j):
         return lax.rem(sub + j, group_devs)
@@ -236,6 +234,8 @@
     for step in range(early):
         to_prev(0, prev_order[step]).start()
         to_next(0, next_order[step]).start()
+    for load in tile_loads:
+        load.start()
     for load in loads[1:]:
         load.wait()
     for j in range(1, group_devs):

time: 69.7 us -> 68.6 us (0.984)
  no operation moved by 1% of the time
where the time goes in v7:
time: 68.6 us; the launch traced here: 68.4 us
  Pallas kernels  66.1 us (96%)
  local copies, waits for them, and re-layouts  2.26 us (3%)
    pallas_call x1, Pallas kernels, per_device(): pl.pallas_call(functools.partial(kernel, groups, group_devs), out_shape=j...  66.1 us
    unnamed x1, local copies, waits for them, and re-layouts  2.26 us

profile of v7, /device:TPU:0, one launch (start us, length us, event | category | flops | bytes accessed | tf_op | source)
XLA Modules:
  0.0 68.4 jit_solution(9133408954902395183)
XLA Ops:
  0.0 66.1 %shard_map.127 = f32[8,256,128]{2,1,0:T(8,128)} custom-call(s32[8,6]{1,0:T(8,128)} %near_hbm.1, s32[4,8]{1,0:T(4,128)} %bitcast.7, s32[1,4]{1,0:T(1,128)} %fdev_hbm.1, s32[1,3]{1,0:T(1,128)} %fmid_hbm.1, f32[8,256,128]{2,1,0:T(8,128)} %bitcast.5, f32[16,128]{1,0:T(8,128)} %bitcast.6, bf16[8,64,256]{2,1,0:T(8,128)(2,1)} %basis_hbm.1, ...), custom_call_target="tpu_custom_call" | custom-call | tf_op jit(solution)/shard_map/pallas_call | solution.py:463
  66.1 2.3 %copy.15 = f32[2048,128]{1,0:T(8,128)} copy(f32[2048,128]{1,0:T(8,128)} %bitcast.4) | data formatting | bytes 2097152
